TPU v7x, 32 devices: a whole 2x2x4 slice. The times are simulated.
32 devices in a mesh: row: 4 (over y, x), col: 8 (over z, core).
Axes of the slice: x: 2, y: 2, z: 4, core: 2. Of those that a mesh axis runs over, the one named last changes fastest.
Arguments:
- tokens: bfloat16 [4096, 4096], P(('row', 'col')), may hold values from -6 to 6
- expert_ids: int32 [4096, 2], P(('row', 'col')), may hold values from 0 to 7, all different within a row; in each aligned block of 128 rows (0 to 127, 128 to 255, ...) at most 40 rows name the same one
- gate_weights: float32 [4096, 2], P(('row', 'col')), may hold values from 0.1 to 1
- w_gate: bfloat16 [8, 4096, 1536], P('col', None, 'row'), may hold values from -0.09375 to 0.09375
- w_up: bfloat16 [8, 4096, 1536], P('col', None, 'row'), may hold values from -0.09375 to 0.09375
- w_down: bfloat16 [8, 1536, 4096], P('col', None, 'row'), may hold values from -0.15625 to 0.15625
Outputs:
- moe_out: bfloat16 [4096, 4096], P(('row', 'col'))
Inputs may be any that keep to these rules, and one draw needn't show every extreme that they name: `expert_ids`: each row names 2 different experts. Among the 128 rows of one device no expert is named by more than 40 rows, and in every draw some expert is named by exactly 40 rows of some device.
All inputs are finite; a program needn't handle non-finite values.
Results may differ from a plain program's by a relative error of at most 0.0058.
Values may be sent and summed in bfloat16 or wider, within the bound.
A program may use at most 128 MiB of HBM per device.

v0:
```python
import jax
import jax.numpy as jnp
from jax import lax
from jax.sharding import PartitionSpec as P


def local(tokens, expert_ids, gate_weights, w_gate, w_up, w_down):
    token_count, top_count = expert_ids.shape
    width = tokens.shape[1]
    local_count = w_gate.shape[0]
    unit_count = w_gate.shape[2]
    quarter = w_down.shape[2]
    columns = lax.axis_size("col")
    groups = lax.axis_size("row")
    experts = local_count * columns
    capacity = max(2, token_count * top_count * 5 // (4 * experts))
    flat_ids = expert_ids.reshape(-1)
    onehot = (flat_ids[:, None] == jnp.arange(experts, dtype=jnp.int32)[None, :]).astype(jnp.int32)
    earlier = jnp.cumsum(onehot, axis=0) - onehot
    position = jnp.sum(earlier * onehot, axis=1)
    slot_ids = (flat_ids * capacity + position).reshape(token_count, top_count)
    chooser = jnp.any(
        jnp.arange(experts * capacity, dtype=jnp.int32)[:, None, None] == slot_ids[None, :, :],
        axis=2,
    ).astype(jnp.bfloat16)
    outgoing = jnp.dot(chooser, tokens, preferred_element_type=jnp.float32).astype(jnp.bfloat16)
    outgoing = outgoing.reshape(columns, local_count * capacity, width)
    arrived = lax.all_to_all(outgoing, "col", split_axis=0, concat_axis=0, tiled=True)
    block_rows = lax.all_gather(arrived[None], "row", axis=0, tiled=True)
    count = block_rows.shape[0]
    grouped = block_rows.reshape(count, columns, local_count, capacity, width)
    expert = 0
    inputs = grouped[:, :, expert].reshape(-1, width)
    gate_part = jnp.dot(inputs, w_gate[expert], preferred_element_type=jnp.float32)
    up_part = jnp.dot(inputs, w_up[expert], preferred_element_type=jnp.float32)
    hidden = (jax.nn.silu(gate_part) * up_part).astype(jnp.bfloat16)
    outputs = hidden.reshape(count, columns, 1, capacity, unit_count)
    hidden_all = outputs.reshape(count, columns, local_count * capacity, unit_count)
    hidden_split = hidden_all.reshape(groups, columns, local_count, capacity, unit_count)
    piece = lax.all_gather(hidden_split, "row", axis=4, tiled=True)
    count = piece.shape[4]
    expert = 0
    rows = piece[:, :, expert].reshape(-1, count)
    block = w_down[expert]
    parts = [jnp.dot(rows, block, preferred_element_type=jnp.float32)]
    summed = jnp.stack(parts)
    expert_out = summed.astype(jnp.bfloat16).reshape(
        local_count, groups, columns, capacity, quarter
    )
    expert_out = jnp.transpose(expert_out, (1, 2, 0, 3, 4)).reshape(
        groups, columns, local_count * capacity, quarter
    )
    colwise = lax.all_to_all(expert_out, "col", split_axis=1, concat_axis=1, tiled=True)
    home = lax.all_to_all(colwise, "row", split_axis=0, concat_axis=3, tiled=True)
    results = home.reshape(experts * capacity, width)
    shares = gate_weights / jnp.sum(gate_weights, axis=1, keepdims=True)
    picked = results[slot_ids].astype(jnp.float32)
    combined = jnp.sum(shares[:, :, None] * picked, axis=1)
    return combined.astype(jnp.bfloat16)


def solution(mesh):
    placed = (
        P(("row", "col"), None),
        P(("row", "col"), None),
        P(("row", "col"), None),
        P("col", None, "row"),
        P("col", None, "row"),
        P("col", None, "row"),
    )
    return jax.shard_map(
        local, mesh=mesh, in_specs=placed, out_specs=P(("row", "col"), None), check_vma=False
    )
```

profile of v0, /device:TPU:19, one launch (start us, length us, event | category | flops | bytes accessed | tf_op | source)
XLA Modules:
  0.0 387.9 jit_solution(17768338284563858844)
XLA Ops:
  6.5 0.9 copy.41
  7.6 0.1 eq.39
  7.8 0.6 reduce-window.6
  8.4 0.2 slice_reduce_fusion
  8.7 0.1 reduce_sum.31
  8.9 0.7 compare_select_fusion
  9.7 2.1 convolution_convert_fusion
  11.7 61.7 %all_to_all.25 = bf16[8,40,4096]{2,1,0:T(8,128)(2,1)} all-to-all(bf16[8,40,4096]{2,1,0:T(8,128)(2,1)S(1)} %bitcast.36), channel_id=1, replica_groups=mesh['row'=4,'col'=8] {'col'}, dimensions={0} | all-to-all | bytes 5242880 | tf_op jit(solution)/shard_map/all_to_all | solution.py:28
  73.5 107.2 %all-gather.6.cloned.1.call-done = bf16[32,40,4096]{2,1,0:T(8,128)(2,1)} async-done(((bf16[8,40,4096]{2,1,0:T(8,128)(2,1)}), bf16[32,40,4096]{2,1,0:T(8,128)(2,1)}) %all-gather.6.cloned.1.call-update) | async-done | bytes 10485776 | tf_op jit(solution)/shard_map/all_gather | solution.py:29
  180.8 9.3 %fusion.2 = f32[1280,384]{1,0:T(8,128)S(1)} fusion(bf16[1280,4096]{1,0:T(8,128)(2,1)} %bitcast.40, bf16[1,4096,384]{2,1,0:T(8,128)(2,1)} %param.9), kind=kOutput, calls=%fused_computation.7 | convolution fusion | flops 4026531840 | bytes 15597568 | tf_op jit(solution)/shard_map/dot_general | solution.py:34
  190.1 6.9 %fusion.4 = bf16[1280,384]{1,0:T(8,128)(2,1)} fusion(bf16[1280,4096]{1,0:T(8,128)(2,1)S(1)} %bitcast.41, bf16[1,4096,384]{2,1,0:T(8,128)(2,1)S(1)} %copy-done.3, f32[1280,384]{1,0:T(8,128)S(1)} %fusion.2), kind=kOutput, calls=%fused_computation.9 | convolution fusion | flops 4029480960 | bytes 16580608 | tf_op jit(solution)/shard_map/dot_general | solution.py:35
  197.1 50.5 %all-gather.4.cloned.1.call-done = bf16[4,8,1,40,1536]{4,3,1,0,2:T(8,128)(2,1)} async-done(((bf16[4,8,1,40,384]{4,3,1,0,2:T(8,128)(2,1)}), bf16[4,8,1,40,1536]{4,3,1,0,2:T(8,128)(2,1)}) %all-gather.4.cloned.1.call-update) | async-done | bytes 3932176 | tf_op jit(solution)/shard_map/all_gather | solution.py:40
  247.6 6.5 %convolution_convert_fusion.1 = bf16[1280,1024]{1,0:T(8,128)(2,1)S(1)} fusion(bf16[1280,1536]{1,0:T(8,128)(2,1)} %bitcast.42, bf16[1,1536,1024]{2,1,0:T(8,128)(2,1)S(1)} %copy-done), kind=kOutput, calls=%fused_computation.3 | convolution fusion | flops 4027842560 | bytes 9699328 | tf_op jit(solution)/shard_map/dot_general | solution.py:45
  254.1 0.3 copy.44
  254.5 61.6 %all_to_all.26 = bf16[4,8,40,1024]{3,2,0,1:T(8,128)(2,1)S(1)} all-to-all(bf16[4,8,40,1024]{3,2,0,1:T(8,128)(2,1)S(1)} %copy.44), channel_id=1, replica_groups=mesh['row'=4,'col'=8] {'col'}, dimensions={1} | all-to-all | bytes 5242880 | tf_op jit(solution)/shard_map/all_to_all | solution.py:53
  316.1 1.8 copy.45
  317.9 4.9 %all-to-all-start.2 = ((bf16[4,8,40,1024]{3,2,1,0:T(8,128)(2,1)}), bf16[4,8,40,1024]{3,2,1,0:T(8,128)(2,1)}, u32[]{:S(2)}, u32[]{:S(2)}) async-start(bf16[4,8,40,1024]{3,2,1,0:T(8,128)(2,1)} %copy.45), calls=%async_computation.2 | async-start | bytes 5242880 | tf_op jit(solution)/shard_map/all_to_all | solution.py:54
  323.0 0.1 reshape.42
  323.3 29.0 %all-to-all-done.2 = bf16[4,8,40,1024]{3,2,1,0:T(8,128)(2,1)} async-done(((bf16[4,8,40,1024]{3,2,1,0:T(8,128)(2,1)}), bf16[4,8,40,1024]{3,2,1,0:T(8,128)(2,1)}, u32[]{:S(2)}, u32[]{:S(2)}) %all-to-all-start.2) | async-done | bytes 2621472 | tf_op jit(solution)/shard_map/all_to_all | solution.py:54
  352.2 3.8 copy.46
  356.0 2.6 copy.48
  358.6 7.3 %gather_fusion = bf16[256,4096]{1,0:T(8,128)(2,1)} fusion(bf16[320,4096]{1,0:T(8,128)(2,1)} %bitcast.35, s32[1024]{0:T(1024)S(1)} %pad_clamp_fusion), kind=kCustom, calls=%fused_computation | custom fusion | bytes 4195328 | tf_op jit(solution)/shard_map/gather | solution.py:57
  365.9 5.4 %reshape.52 = f32[128,2,4096]{2,1,0:T(2,128)} reshape(bf16[256,4096]{1,0:T(8,128)(2,1)} %gather_fusion) | data formatting | bytes 6291456 | tf_op jit(solution)/shard_map/convert_element_type | solution.py:57
  371.4 9.6 %multiply_reduce_fusion = bf16[128,4096]{1,0:T(8,128)(2,1)} fusion(f32[128,2,4096]{2,1,0:T(2,128)} %reshape.52, f32[128,2]{1,0:T(8,128)S(1)} %copy.40), kind=kLoop, calls=%fused_computation.2 | loop fusion | flops 1572864 | bytes 5243904 | tf_op jit(solution)/shard_map/reduce_sum | solution.py:58
  (24 shorter events, 0.7 us)
Async XLA Ops:
  6.5 241.0 %copy-start = (bf16[1,1536,1024]{2,1,0:T(8,128)(2,1)S(1)}, bf16[1,1536,1024]{2,1,0:T(8,128)(2,1)}, u32[]{:S(2)}) copy-start(bf16[1,1536,1024]{2,1,0:T(8,128)(2,1)} %param.11) | copy-start | bytes 9437188
  6.5 174.2 %all-gather.6.cloned.1.call-start = ((), (), s32[]{:S(2)}) async-start(), calls=%async_computation.4 | async-start | bytes 13107200 | tf_op jit(solution)/shard_map/all_gather | solution.py:29
  73.5 174.1 %all-gather.4.cloned.1.call-start = ((), (), s32[]{:S(2)}) async-start(), calls=%async_computation.3 | async-start | bytes 4915200 | tf_op jit(solution)/shard_map/all_gather | solution.py:40
  180.8 9.4 %copy-start.2 = (bf16[32,40,4096]{2,1,0:T(8,128)(2,1)S(1)}, bf16[32,40,4096]{2,1,0:T(8,128)(2,1)}, u32[]{:S(2)}) copy-start(bf16[32,40,4096]{2,1,0:T(8,128)(2,1)} %all-gather.6.cloned.1.call-done) | copy-start | bytes 31457284
  180.8 9.4 %copy-start.3 = (bf16[1,4096,384]{2,1,0:T(8,128)(2,1)S(1)}, bf16[1,4096,384]{2,1,0:T(8,128)(2,1)}, u32[]{:S(2)}) copy-start(bf16[1,4096,384]{2,1,0:T(8,128)(2,1)} %param.10) | copy-start | bytes 9437188
  317.9 5.2 %copy-start.1 = (f32[128,2]{0,1:T(2,128)S(1)}, f32[128,2]{0,1:T(2,128)}, u32[]{:S(2)}) copy-start(f32[128,2]{0,1:T(2,128)} %param.8) | copy-start | bytes 3076
  317.9 34.3 %all-to-all-start.2 = ((bf16[4,8,40,1024]{3,2,1,0:T(8,128)(2,1)}), bf16[4,8,40,1024]{3,2,1,0:T(8,128)(2,1)}, u32[]{:S(2)}, u32[]{:S(2)}) async-start(bf16[4,8,40,1024]{3,2,1,0:T(8,128)(2,1)} %copy.45), calls=%async_computation.2 | async-start | bytes 5242880 | tf_op jit(solution)/shard_map/all_to_all | solution.py:54
Sparse Core Ops, SparseCore 0:
  73.6 107.1 all-gather.5
  197.2 50.3 all-gather.3
where the time goes:
time: 394 us; the launch traced here: 388 us
  waiting for transfers between devices  187 us (47%)
  blocking collectives  123 us (31%)
  matrix products  24.9 us (6%)
  local copies, waits for them, and re-layouts  23.3 us (6%)
  between operations  13.5 us (3%)
  other arithmetic  11.1 us (3%)
  starting transfers between devices  4.98 us (1%)
    all_gather x1, waiting for transfers between devices, local(): block_rows = lax.all_gather(arrived[None], 'row', axis=0, tiled=True)  107 us
    all_to_all x1, blocking collectives, local(): lax.all_to_all(outgoing, 'col', split_axis=0, concat_axis=0, tiled=True)  61.7 us
    all_to_all x1, blocking collectives, local(): lax.all_to_all(expert_out, 'col', split_axis=1, concat_axis=1, tiled=True)  61.6 us
    all_gather x1, waiting for transfers between devices, local(): piece = lax.all_gather(hidden_split, 'row', axis=4, tiled=True)  50.5 us
    all_to_all x1, waiting for transfers between devices, local(): lax.all_to_all(colwise, 'row', split_axis=0, concat_axis=3, tiled=True)  29 us
    reduce_sum x1, other arithmetic, local(): combined = jnp.sum(shares[:, :, None] * picked, axis=1)  9.64 us
    dot_general x1, matrix products, local(): jnp.dot(inputs, w_gate[expert], preferred_element_type=jnp.float32)  9.34 us
  transfers between devices with their start and end apart: 3, of which 3 were waited for; matrix products, arithmetic and copies ran while one was open for 0% of the time, Pallas kernels for 0%

commit v1 on v0

--- a/solution.py
+++ b/solution.py
@@ -1,7 +1,247 @@
+import functools
+
 import jax
 import jax.numpy as jnp
 from jax import lax
+from jax.experimental import pallas as pl
+from jax.experimental.pallas import tpu as pltpu
 from jax.sharding import PartitionSpec as P
+
+MESH = pl.DeviceIdType.MESH
+F32 = jnp.float32
+BF16 = jnp.bfloat16
+
+
+def flip(value, mask):
+    bit = 1
+    while bit <= mask:
+        if mask & bit:
+            value = value + bit * (1 - 2 * lax.rem(lax.div(value, bit), 2))
+        bit *= 2
+    return value
+
+
+def kernel(
+    ids_ref, gate_ref, tok_ref, wg_ref, wu_ref, wd_ref, out_ref,
+    outg, rows, w, wd, acc, hid, part, res, pick,
+    w_sem, z_send, z_recv, x_send, x_recv, y_send, y_recv, d_send, d_recv,
+    h_send, h_recv, r_send, r_recv,
+):
+    row, col = lax.axis_index("row"), lax.axis_index("col")
+    columns, groups, cap, width = rows.shape
+    tokens = tok_ref.shape[0]
+    units = wg_ref.shape[2]
+    quarter = wd_ref.shape[2]
+    steps = columns // 2
+    slots = columns * cap
+    span = 2 * groups * cap
+
+    def peer(k, m):
+        return (flip(row, k), flip(col, m))
+
+    barrier = pltpu.get_barrier_semaphore()
+    for k in range(groups):
+        for m in range(columns):
+            if k or m:
+                pl.semaphore_signal(barrier, inc=1, device_id=peer(k, m), device_id_type=MESH)
+
+    loads = [
+        pltpu.make_async_copy(wg_ref.at[0], w.at[:, pl.ds(0, units)], w_sem.at[0]),
+        pltpu.make_async_copy(wu_ref.at[0], w.at[:, pl.ds(units, units)], w_sem.at[1]),
+    ]
+    for k in range(groups):
+        start = pl.multiple_of(flip(row, k) * units, units)
+        loads.append(
+            pltpu.make_async_copy(wd_ref.at[0, pl.ds(start, units)], wd.at[k], w_sem.at[2 + k])
+        )
+    for load in loads:
+        load.start()
+
+    ids = ids_ref[...]
+    block = lax.broadcasted_iota(jnp.int32, (columns, tokens), 0)
+    named = [(ids[k : k + 1, :] == block).astype(F32) for k in range(2)]
+    before = (
+        lax.broadcasted_iota(jnp.int32, (tokens, tokens), 0)
+        < lax.broadcasted_iota(jnp.int32, (tokens, tokens), 1)
+    ).astype(F32).astype(BF16)
+    place = jnp.dot((named[0] + named[1]).astype(BF16), before, preferred_element_type=F32)
+    place = place.astype(jnp.int32)
+    slot = lax.broadcasted_iota(jnp.int32, (columns, cap, tokens), 1)
+    hit = place[:, None, :] == slot
+    chosen = [jnp.where(hit, n[:, None, :], 0.0).reshape(slots, tokens) for n in named]
+    for k in range(2):
+        pick[k] = chosen[k].astype(BF16)
+    both = (chosen[0] + chosen[1]).astype(BF16)
+    tile = 512
+    for j in range(width // tile):
+        at = pl.ds(j * tile, tile)
+        sent = jnp.dot(both, tok_ref[:, at], preferred_element_type=F32)
+        sent = sent.reshape(columns, cap, tile).astype(BF16)
+        rows[0, 0, :, at] = sent[0]
+        outg[:, :, at] = sent[1:]
+
+    def remote(src, dst, send, recv, k, m):
+        return pltpu.make_async_remote_copy(
+            src_ref=src, dst_ref=dst, send_sem=send, recv_sem=recv,
+            device_id=peer(k, m), device_id_type=MESH,
+        )
+
+    zc = {
+        m: remote(outg.at[m - 1], rows.at[m, 0], z_send.at[m - 1], z_recv.at[m - 1], 0, m)
+        for m in range(1, columns)
+    }
+    xc = [remote(rows.at[m, 0], rows.at[m, 1], x_send.at[m], x_recv.at[m], 1, 0) for m in range(columns)]
+    yc = [remote(rows.at[m, 0], rows.at[m, 2], y_send.at[m], y_recv.at[m], 2, 0) for m in range(columns)]
+    dc = [
+        remote(rows.at[m, 1 + m % 2], rows.at[m, 3], d_send.at[m], d_recv.at[m], 2 - m % 2, 0)
+        for m in range(columns)
+    ]
+    hx = [remote(hid.at[0, g], hid.at[1, g], h_send.at[g, 0], h_recv.at[g, 0], 1, 0) for g in range(steps)]
+    hy = [remote(hid.at[0, g], hid.at[2, g], h_send.at[g, 1], h_recv.at[g, 1], 2, 0) for g in range(steps)]
+    hd = [
+        remote(hid.at[1 + g % 2, g], hid.at[3, g], h_send.at[g, 2], h_recv.at[g, 2], 2 - g % 2, 0)
+        for g in range(steps)
+    ]
+    rc = {
+        (m, k): remote(part.at[m, k], res.at[k, m], r_send.at[m, k], r_recv.at[m, k], k, m)
+        for m in range(columns) for k in range(groups) if k or m
+    }
+
+    pl.semaphore_wait(barrier, groups * columns - 1)
+
+    def stage_a(g):
+        for m in (2 * g, 2 * g + 1):
+            if m:
+                zc[m].wait_recv()
+            xc[m].start()
+            yc[m].start()
+
+    def stage_b(g):
+        for m in (2 * g, 2 * g + 1):
+            xc[m].wait_recv()
+            yc[m].wait_recv()
+            dc[m].start()
+
+    def stage_c(g):
+        for m in (2 * g, 2 * g + 1):
+            dc[m].wait_recv()
+        if g == 0:
+            loads[0].wait()
+            loads[1].wait()
+        acc[...] = jnp.zeros_like(acc)
+        depth = 512
+
+        def body(i, carry):
+            at = pl.ds(pl.multiple_of(i * depth, depth), depth)
+            lhs = rows[2 * g : 2 * g + 2, :, :, at].reshape(span, depth)
+            acc[...] += jnp.dot(lhs, w[at, :], preferred_element_type=F32)
+            return carry
+
+        lax.fori_loop(0, width // depth, body, 0)
+        gate, up = acc[:, :units], acc[:, units:]
+        hid[0, g] = (gate / (1.0 + jnp.exp(-gate)) * up).astype(BF16)
+        hx[g].start()
+        hy[g].start()
+
+    def stage_d(g):
+        hx[g].wait_recv()
+        hy[g].wait_recv()
+        hd[g].start()
+
+    def stage_e(g):
+        hd[g].wait_recv()
+        if g == 0:
+            for load in loads[2:]:
+                load.wait()
+        wide = 256
+
+        def body(i, carry):
+            at = pl.ds(pl.multiple_of(i * wide, wide), wide)
+            total = [None] * groups
+            for q in range(groups):
+                out = jnp.dot(hid[q, g], wd[q, :, at], preferred_element_type=F32)
+                out = out.reshape(2, groups, cap, wide)
+                for k in range(groups):
+                    term = out[:, k]
+                    total[k ^ q] = term if total[k ^ q] is None else total[k ^ q] + term
+            for k in range(groups):
+                part[2 * g : 2 * g + 2, k, :, at] = total[k].astype(BF16)
+            if g == 0:
+                res[0, 0, :, at] = total[0][0].astype(BF16)
+            return carry
+
+        lax.fori_loop(0, quarter // wide, body, 0)
+        for m in (2 * g, 2 * g + 1):
+            for k in range(groups):
+                if k or m:
+                    rc[m, k].start()
+
+    for m in range(1, columns):
+        zc[m].start()
+    for turn in range(steps + 4):
+        for offset, stage in enumerate((stage_a, stage_b, stage_c, stage_d, stage_e)):
+            if 0 <= turn - offset < steps:
+                stage(turn - offset)
+
+    share = gate_ref[...]
+    share = share / jnp.sum(share, axis=1, keepdims=True)
+    for copy in rc.values():
+        copy.wait_recv()
+    for k in range(groups):
+        got = res[k].reshape(slots, quarter)
+        total = None
+        for choice in range(2):
+            term = lax.dot_general(
+                pick[choice], got, (((0,), (0,)), ((), ())), preferred_element_type=F32
+            )
+            term = share[:, choice : choice + 1] * term
+            total = term if total is None else total + term
+        at = pl.ds(pl.multiple_of(flip(row, k) * quarter, quarter), quarter)
+        out_ref[:, at] = total.astype(BF16)
+
+    for copy in [*zc.values(), *xc, *yc, *dc, *hx, *hy, *hd, *rc.values()]:
+        copy.wait_send()
+
+
+def fused(tokens, expert_ids, gate_weights, w_gate, w_up, w_down, cap):
+    columns, groups = lax.axis_size("col"), lax.axis_size("row")
+    count, width = tokens.shape
+    units, quarter = w_gate.shape[2], w_down.shape[2]
+    ids = expert_ids.T ^ lax.axis_index("col")
+    dma = pltpu.SemaphoreType.DMA
+    vmem = pl.BlockSpec(memory_space=pltpu.VMEM)
+    hbm = pl.BlockSpec(memory_space=pl.ANY)
+    slots = columns * cap
+    return pl.pallas_call(
+        kernel,
+        out_shape=jax.ShapeDtypeStruct((count, width), BF16),
+        in_specs=[vmem] * 3 + [hbm] * 3,
+        out_specs=vmem,
+        scratch_shapes=[
+            pltpu.VMEM((columns - 1, cap, width), BF16),
+            pltpu.VMEM((columns, groups, cap, width), BF16),
+            pltpu.VMEM((width, 2 * units), BF16),
+            pltpu.VMEM((groups, units, quarter), BF16),
+            pltpu.VMEM((2 * groups * cap, 2 * units), F32),
+            pltpu.VMEM((groups, columns // 2, 2 * groups * cap, units), BF16),
+            pltpu.VMEM((columns, groups, cap, quarter), BF16),
+            pltpu.VMEM((groups, columns, cap, quarter), BF16),
+            pltpu.VMEM((2, slots, count), BF16),
+            dma((2 + groups,)),
+            dma((columns - 1,)), dma((columns - 1,)),
+            dma((columns,)), dma((columns,)),
+            dma((columns,)), dma((columns,)),
+            dma((columns,)), dma((columns,)),
+            dma((columns // 2, 3)), dma((columns // 2, 3)),
+            dma((columns, groups)), dma((columns, groups)),
+        ],
+        compiler_params=pltpu.CompilerParams(
+            collective_id=0, has_side_effects=True, vmem_limit_bytes=60 * 2**20
+        ),
+        cost_estimate=pl.CostEstimate(
+            flops=2 * slots * groups * width * units * 3, bytes_accessed=12 * 2**20, transcendentals=0
+        ),
+    )(ids, gate_weights, tokens, w_gate, w_up, w_down)
 
 
 def local(tokens, expert_ids, gate_weights, w_gate, w_up, w_down):
@@ -14,9 +254,13 @@
     groups = lax.axis_size("row")
     experts = local_count * columns
     capacity = max(2, token_count * top_count * 5 // (4 * experts))
+    if groups == 4 and columns == 8 and local_count == 1 and top_count == 2 and capacity % 8 == 0:
+        return fused(tokens, expert_ids, gate_weights, w_gate, w_up, w_down, capacity)
     flat_ids = expert_ids.reshape(-1)
     onehot = (flat_ids[:, None] == jnp.arange(experts, dtype=jnp.int32)[None, :]).astype(jnp.int32)
-    earlier = jnp.cumsum(onehot, axis=0) - onehot
+    entries = jnp.arange(flat_ids.shape[0], dtype=jnp.int32)
+    before = (entries[None, :] < entries[:, None]).astype(jnp.bfloat16)
+    earlier = jnp.dot(before, onehot.astype(jnp.bfloat16), preferred_element_type=jnp.float32).astype(jnp.int32)
     position = jnp.sum(earlier * onehot, axis=1)
     slot_ids = (flat_ids * capacity + position).reshape(token_count, top_count)
     chooser = jnp.any(

time: 394 us -> 200 us (0.51); the launches traced: 388 us -> 200 us
  Pallas kernels: 0 us -> 195 us
  waiting for transfers between devices: 187 us -> 0 us
  blocking collectives: 123 us -> 0 us
  matrix products: 24.9 us -> 0 us
  local copies, waits for them, and re-layouts: 23.3 us -> 3.7 us
  between operations: 13.5 us -> 0.01 us
  other arithmetic: 11.1 us -> 1.27 us
  starting transfers between devices: 4.98 us -> 0 us
    pallas_call x0 -> x1, Pallas kernels: none -> 195 us  [fused(): pl.pallas_call(kernel, out_shape=jax.ShapeDtypeStruct((count, width), BF1...]
    all_gather x2 -> x0, waiting for transfers between devices: 158 us -> none  [the longest x1 107 us: local(): block_rows = lax.all_gather(arrived[None], 'row', axis=0, tiled=True)]
    all_to_all x2 -> x0, blocking collectives: 123 us -> none  [the longest x1 61.7 us: local(): lax.all_to_all(outgoing, 'col', split_axis=0, concat_axis=0, tiled=True)]
    all_to_all x1 -> x0, waiting for transfers between devices: 29 us -> none  [local(): lax.all_to_all(colwise, 'row', split_axis=0, concat_axis=3, tiled=True)]
    dot_general x4 -> x0, matrix products: 24.9 us -> none  [the longest x1 9.34 us: local(): jnp.dot(inputs, w_gate[expert], preferred_element_type=jnp.float32)]
    reduce_sum x3 -> x0, other arithmetic: 9.75 us -> none  [the longest x1 9.64 us: local(): combined = jnp.sum(shares[:, :, None] * picked, axis=1)]
    gather x1 -> x0, local copies, waits for them, and re-layouts: 7.29 us -> none  [local(): picked = results[slot_ids].astype(jnp.float32)]
    all_to_all x2 -> x0, local copies, waits for them, and re-layouts: 5.57 us -> none  [the longest x1 3.77 us: local(): lax.all_to_all(colwise, 'row', split_axis=0, concat_axis=3, tiled=True)]
  transfers between devices with their start and end apart: 3 -> 0, of which waited for: 3 -> 0; matrix products, arithmetic and copies ran while one was open for 0% -> 0% of each run, Pallas kernels for 0% -> 0%
where the time goes in v1:
time: 200 us
  Pallas kernels  195 us (98%)
  local copies, waits for them, and re-layouts  3.7 us (2%)
    pallas_call x1, Pallas kernels, fused(): pl.pallas_call(kernel, out_shape=jax.ShapeDtypeStruct((count, width), BF1...  195 us

profile of v1, /device:TPU:19, one launch (start us, length us, event | category | flops | bytes accessed | tf_op | source)
XLA Modules:
  0.0 200.0 jit_solution(1059280571986149569)
XLA Ops:
  0.0 1.3 xor_bitcast_fusion.ids_ref
  1.3 1.4 copy.7.gate_ref
  2.7 195.0 %shard_map.64 = bf16[128,4096]{1,0:T(8,128)(2,1)} custom-call(s32[2,128]{1,0:T(2,128)} %xor_bitcast_fusion.ids_ref, f32[128,2]{1,0:T(8,128)} %copy.7.gate_ref, bf16[128,4096]{1,0:T(8,128)(2,1)} %tok_ref.1, bf16[1,4096,384]{2,1,0:T(8,128)(2,1)} %wg_ref.1, bf16[1,4096,384]{2,1,0:T(8,128)(2,1)} %wu_ref.1, bf16[1,1536,1024]{2,1,0:T(8,128)(2,1)} %wd_ref.1), custom_call_target="tpu_custom_call" | custom-call | flops 12079595520 | bytes 12582912 | tf_op jit(solution)/shard_map/pallas_call | solution.py:215
  197.7 2.3 %copy.9 = bf16[128,4096]{1,0:T(8,128)(2,1)} copy(bf16[128,4096]{1,0:T(8,128)(2,1)} %shard_map.64) | data formatting | bytes 2097152

commit v2 on v1

--- a/solution.py
+++ b/solution.py
@@ -8,6 +8,11 @@
 from jax.sharding import PartitionSpec as P
 
 MESH = pl.DeviceIdType.MESH
+ORDER = (0, 1, 2, 3, 4, 5, 6, 7)
+SIZES = (1,)*8
+LAGS = (0, 1, 2, 3, 4)
+NEWEST_FIRST = False
+AHEAD = 99
 F32 = jnp.float32
 BF16 = jnp.bfloat16
 
@@ -32,9 +37,9 @@
     tokens = tok_ref.shape[0]
     units = wg_ref.shape[2]
     quarter = wd_ref.shape[2]
-    steps = columns // 2
+    steps = len(SIZES)
+    firsts = [sum(SIZES[:g]) for g in range(steps)]
     slots = columns * cap
-    span = 2 * groups * cap
 
     def peer(k, m):
         return (flip(row, k), flip(col, m))
@@ -59,7 +64,10 @@
 
     ids = ids_ref[...]
     block = lax.broadcasted_iota(jnp.int32, (columns, tokens), 0)
-    named = [(ids[k : k + 1, :] == block).astype(F32) for k in range(2)]
+    masks = jnp.zeros_like(block)
+    for p, m in enumerate(ORDER):
+        masks = jnp.where(block == p, m, masks)
+    named = [(ids[k : k + 1, :] == masks).astype(F32) for k in range(2)]
     before = (
         lax.broadcasted_iota(jnp.int32, (tokens, tokens), 0)
         < lax.broadcasted_iota(jnp.int32, (tokens, tokens), 1)
@@ -87,7 +95,7 @@
         )
 
     zc = {
-        m: remote(outg.at[m - 1], rows.at[m, 0], z_send.at[m - 1], z_recv.at[m - 1], 0, m)
+        m: remote(outg.at[m - 1], rows.at[m, 0], z_send.at[m - 1], z_recv.at[m - 1], 0, ORDER[m])
         for m in range(1, columns)
     }
     xc = [remote(rows.at[m, 0], rows.at[m, 1], x_send.at[m], x_recv.at[m], 1, 0) for m in range(columns)]
@@ -96,50 +104,56 @@
         remote(rows.at[m, 1 + m % 2], rows.at[m, 3], d_send.at[m], d_recv.at[m], 2 - m % 2, 0)
         for m in range(columns)
     ]
-    hx = [remote(hid.at[0, g], hid.at[1, g], h_send.at[g, 0], h_recv.at[g, 0], 1, 0) for g in range(steps)]
-    hy = [remote(hid.at[0, g], hid.at[2, g], h_send.at[g, 1], h_recv.at[g, 1], 2, 0) for g in range(steps)]
-    hd = [
-        remote(hid.at[1 + g % 2, g], hid.at[3, g], h_send.at[g, 2], h_recv.at[g, 2], 2 - g % 2, 0)
-        for g in range(steps)
-    ]
+
+    def units_copy(g, source, target, number, k):
+        at = pl.ds(firsts[g], SIZES[g])
+        return remote(
+            hid.at[source, at], hid.at[target, at], h_send.at[g, number], h_recv.at[g, number], k, 0
+        )
+
+    hx = [units_copy(g, 0, 1, 0, 1) for g in range(steps)]
+    hy = [units_copy(g, 0, 2, 1, 2) for g in range(steps)]
+    hd = [units_copy(g, 1 + g % 2, 3, 2, 2 - g % 2) for g in range(steps)]
     rc = {
-        (m, k): remote(part.at[m, k], res.at[k, m], r_send.at[m, k], r_recv.at[m, k], k, m)
+        (m, k): remote(part.at[m, k], res.at[k, m], r_send.at[m, k], r_recv.at[m, k], k, ORDER[m])
         for m in range(columns) for k in range(groups) if k or m
     }
 
     pl.semaphore_wait(barrier, groups * columns - 1)
 
     def stage_a(g):
-        for m in (2 * g, 2 * g + 1):
+        for m in range(firsts[g], firsts[g] + SIZES[g]):
             if m:
                 zc[m].wait_recv()
             xc[m].start()
             yc[m].start()
 
     def stage_b(g):
-        for m in (2 * g, 2 * g + 1):
+        for m in range(firsts[g], firsts[g] + SIZES[g]):
             xc[m].wait_recv()
             yc[m].wait_recv()
             dc[m].start()
 
     def stage_c(g):
-        for m in (2 * g, 2 * g + 1):
+        for m in range(firsts[g], firsts[g] + SIZES[g]):
             dc[m].wait_recv()
         if g == 0:
             loads[0].wait()
             loads[1].wait()
-        acc[...] = jnp.zeros_like(acc)
+        span = SIZES[g] * groups * cap
+        acc[:span] = jnp.zeros((span, 2 * units), F32)
         depth = 512
 
         def body(i, carry):
             at = pl.ds(pl.multiple_of(i * depth, depth), depth)
-            lhs = rows[2 * g : 2 * g + 2, :, :, at].reshape(span, depth)
-            acc[...] += jnp.dot(lhs, w[at, :], preferred_element_type=F32)
+            lhs = rows[firsts[g] : firsts[g] + SIZES[g], :, :, at].reshape(span, depth)
+            acc[:span] += jnp.dot(lhs, w[at, :], preferred_element_type=F32)
             return carry
 
         lax.fori_loop(0, width // depth, body, 0)
-        gate, up = acc[:, :units], acc[:, units:]
-        hid[0, g] = (gate / (1.0 + jnp.exp(-gate)) * up).astype(BF16)
+        gate, up = acc[:span, :units], acc[:span, units:]
+        value = (gate / (1.0 + jnp.exp(-gate)) * up).astype(BF16)
+        hid[0, firsts[g] : firsts[g] + SIZES[g]] = value.reshape(SIZES[g], groups * cap, units)
         hx[g].start()
         hy[g].start()
 
@@ -159,29 +173,35 @@
             at = pl.ds(pl.multiple_of(i * wide, wide), wide)
             total = [None] * groups
             for q in range(groups):
-                out = jnp.dot(hid[q, g], wd[q, :, at], preferred_element_type=F32)
-                out = out.reshape(2, groups, cap, wide)
+                left = hid[q, firsts[g] : firsts[g] + SIZES[g]].reshape(-1, units)
+                out = jnp.dot(left, wd[q, :, at], preferred_element_type=F32)
+                out = out.reshape(SIZES[g], groups, cap, wide)
                 for k in range(groups):
                     term = out[:, k]
                     total[k ^ q] = term if total[k ^ q] is None else total[k ^ q] + term
             for k in range(groups):
-                part[2 * g : 2 * g + 2, k, :, at] = total[k].astype(BF16)
+                part[firsts[g] : firsts[g] + SIZES[g], k, :, at] = total[k].astype(BF16)
             if g == 0:
                 res[0, 0, :, at] = total[0][0].astype(BF16)
             return carry
 
         lax.fori_loop(0, quarter // wide, body, 0)
-        for m in (2 * g, 2 * g + 1):
+        for m in range(firsts[g], firsts[g] + SIZES[g]):
             for k in range(groups):
                 if k or m:
                     rc[m, k].start()
 
-    for m in range(1, columns):
-        zc[m].start()
-    for turn in range(steps + 4):
-        for offset, stage in enumerate((stage_a, stage_b, stage_c, stage_d, stage_e)):
-            if 0 <= turn - offset < steps:
-                stage(turn - offset)
+    stages = list(enumerate((stage_a, stage_b, stage_c, stage_d, stage_e)))
+    if not NEWEST_FIRST:
+        stages.reverse()
+    begun = 1
+    for turn in range(steps + LAGS[-1]):
+        while begun < columns and begun < sum(SIZES[: turn + 1 + AHEAD]):
+            zc[begun].start()
+            begun += 1
+        for number, stage in stages:
+            if 0 <= turn - LAGS[number] < steps:
+                stage(turn - LAGS[number])
 
     share = gate_ref[...]
     share = share / jnp.sum(share, axis=1, keepdims=True)
@@ -222,8 +242,8 @@
             pltpu.VMEM((columns, groups, cap, width), BF16),
             pltpu.VMEM((width, 2 * units), BF16),
             pltpu.VMEM((groups, units, quarter), BF16),
-            pltpu.VMEM((2 * groups * cap, 2 * units), F32),
-            pltpu.VMEM((groups, columns // 2, 2 * groups * cap, units), BF16),
+            pltpu.VMEM((max(SIZES) * groups * cap, 2 * units), F32),
+            pltpu.VMEM((groups, columns, groups * cap, units), BF16),
             pltpu.VMEM((columns, groups, cap, quarter), BF16),
             pltpu.VMEM((groups, columns, cap, quarter), BF16),
             pltpu.VMEM((2, slots, count), BF16),
@@ -232,7 +252,7 @@
             dma((columns,)), dma((columns,)),
             dma((columns,)), dma((columns,)),
             dma((columns,)), dma((columns,)),
-            dma((columns // 2, 3)), dma((columns // 2, 3)),
+            dma((len(SIZES), 3)), dma((len(SIZES), 3)),
             dma((columns, groups)), dma((columns, groups)),
         ],
         compiler_params=pltpu.CompilerParams(

time: 200 us -> 188 us (0.940)
  Pallas kernels: 195 us -> 182 us
    pallas_call x1, Pallas kernels: 195 us -> 182 us  [fused(): pl.pallas_call(kernel, out_shape=jax.ShapeDtypeStruct((count, width), BF1...]
where the time goes in v2:
time: 188 us; the launch traced here: 187 us
  Pallas kernels  182 us (97%)
  local copies, waits for them, and re-layouts  3.7 us (2%)
    pallas_call x1, Pallas kernels, fused(): pl.pallas_call(kernel, out_shape=jax.ShapeDtypeStruct((count, width), BF1...  182 us

profile of v2, /device:TPU:19, one launch (start us, length us, event | category | flops | bytes accessed | tf_op | source)
XLA Modules:
  0.0 187.3 jit_solution(9535300666424655480)
XLA Ops:
  0.0 1.3 xor_bitcast_fusion.ids_ref
  1.3 1.4 copy.7.gate_ref
  2.7 182.3 %shard_map.64 = bf16[128,4096]{1,0:T(8,128)(2,1)} custom-call(s32[2,128]{1,0:T(2,128)} %xor_bitcast_fusion.ids_ref, f32[128,2]{1,0:T(8,128)} %copy.7.gate_ref, bf16[128,4096]{1,0:T(8,128)(2,1)} %tok_ref.1, bf16[1,4096,384]{2,1,0:T(8,128)(2,1)} %wg_ref.1, bf16[1,4096,384]{2,1,0:T(8,128)(2,1)} %wu_ref.1, bf16[1,1536,1024]{2,1,0:T(8,128)(2,1)} %wd_ref.1), custom_call_target="tpu_custom_call" | custom-call | flops 12079595520 | bytes 12582912 | tf_op jit(solution)/shard_map/pallas_call | solution.py:235
  185.0 2.3 %copy.9 = bf16[128,4096]{1,0:T(8,128)(2,1)} copy(bf16[128,4096]{1,0:T(8,128)(2,1)} %shard_map.64) | data formatting | bytes 2097152
